TPU v7x, 32 devices: a whole 2x2x4 slice. The times are simulated.
32 devices in a mesh: dp: 2 (over core), modes: 16 (over z, y, x).
Axes of the slice: x: 2, y: 2, z: 4, core: 2. Of those that a mesh axis runs over, the one named last changes fastest.
Arguments:
- x_in: bfloat16 [32768, 512], P(('dp', 'modes')), may hold values from -6 to 6
- cotangent: bfloat16 [32768, 512], P(('dp', 'modes')), may hold values from -6 to 6
- block_grid: int32 [512], P(('dp', 'modes')), may hold values from 8 to 32, as said below
- keep_modes: int32 [3], replicated, may hold values from 6 to 32, as said below
- norm1_gain: float32 [2, 512], replicated, may hold values from 0.5 to 1.5
- norm1_bias: float32 [2, 512], replicated, may hold values from -1.8 to 1.8
- mix_w1: bfloat16 [2, 2, 8, 64, 64], replicated, may hold values from -0.5 to 0.5
- mix_b1: float32 [2, 2, 512], replicated, may hold values from -3 to 3
- mix_w2: bfloat16 [2, 2, 8, 64, 64], replicated, may hold values from -0.5 to 0.5
- mix_b2: float32 [2, 2, 512], replicated, may hold values from -1.8 to 1.8
- norm2_gain: float32 [2, 512], replicated, may hold values from 0.5 to 1.5
- norm2_bias: float32 [2, 512], replicated, may hold values from -1.8 to 1.8
- fc1: bfloat16 [2, 512, 512], replicated, may hold values from -0.25 to 0.25
- fc1_bias: float32 [2, 512], replicated, may hold values from -1.8 to 1.8
- fc2: bfloat16 [2, 512, 512], replicated, may hold values from -0.375 to 0.375
- fc2_bias: float32 [2, 512], replicated, may hold values from -1.8 to 1.8
Outputs:
- out: bfloat16 [32768, 512], P(('dp', 'modes'))
- x_grad: bfloat16 [32768, 512], P(('dp', 'modes'))
- norm1_gain_grad: float32 [2, 512], replicated
- norm1_bias_grad: float32 [2, 512], replicated
- mix_w1_grad: float32 [2, 2, 8, 64, 64], replicated
- mix_b1_grad: float32 [2, 2, 512], replicated
- mix_w2_grad: float32 [2, 2, 8, 64, 64], replicated
- mix_b2_grad: float32 [2, 2, 512], replicated
- norm2_gain_grad: float32 [2, 512], replicated
- norm2_bias_grad: float32 [2, 512], replicated
- fc1_grad: float32 [2, 512, 512], replicated
- fc1_bias_grad: float32 [2, 512], replicated
- fc2_grad: float32 [2, 512, 512], replicated
- fc2_bias_grad: float32 [2, 512], replicated
Inputs may be any that keep to these rules, and one draw needn't show every extreme that they name: `block_grid`: each slab's 16 entries are all 32, or four quarters of 4 entries, each quarter all 16 or all 8; some slab is all 32 and some quarter is all 8. `keep_modes`: entry 0 is 8 minus a quarter of it (rounded down), entry 2 is 32, entry 1 lies between 16 minus a quarter of it (rounded down) and 16.
All inputs are finite; a program needn't handle non-finite values.
Results may differ from a plain program's by a relative error of at most 0.019.
Values may be sent and summed in bfloat16 or wider, within the bound.
No kernel may reach another device: no remote copies, remote signals or barrier semaphores. Data moves between devices by JAX's collectives and lax.ppermute only.
A program may use at most 192 MiB of HBM per device.

v0:
```python
from functools import partial

import jax
import jax.numpy as jnp
from jax import lax
from jax.sharding import PartitionSpec as P

BLOCKS = 8
GS = 8
GM = 16
NBLK = 16
LAYERS = 2


def dft_tables(grid_blocks, keep, slab_rows):
    rows = jnp.arange(slab_rows, dtype=jnp.int32)
    count = grid_blocks.shape[0]
    blk = rows // (slab_rows // count)
    match = (blk[:, None] == jnp.arange(count, dtype=jnp.int32)[None, :]).astype(jnp.int32)
    grid = jnp.sum(match * grid_blocks[None, :], axis=1)
    span = grid * grid
    start = rows // span * span
    local = rows - start
    prow = local // grid
    pcol = local % grid
    keep_now = jnp.where(grid == GS, keep[0], jnp.where(grid == GM, keep[1], keep[2]))
    used = (prow < keep_now) & (pcol < keep_now)
    same = start[:, None] == start[None, :]
    phase = (prow[:, None] * prow[None, :] + pcol[:, None] * pcol[None, :]) % grid[:, None]
    sidef = grid.astype(jnp.float32)[:, None]
    angle = phase.astype(jnp.float32) * (2.0 * jnp.pi) / sidef
    live = same & used[:, None]
    table_re = jnp.where(live, jnp.cos(angle) / sidef, jnp.float32(0.0))
    table_im = jnp.where(live, -jnp.sin(angle) / sidef, jnp.float32(0.0))
    return (table_re.astype(jnp.bfloat16), table_im.astype(jnp.bfloat16))


def layer_norm(x, gain, shift):
    mean = jnp.mean(x, -1, keepdims=True)
    cent = x - mean
    var = jnp.mean(cent * cent, -1, keepdims=True)
    return cent * lax.rsqrt(var + 1e-05) * gain + shift


def shrink(v):
    return v - 0.05 * v * lax.rsqrt(v * v + 0.0025)


def spectral(table, x):
    slabs = table.shape[0]
    out = jnp.einsum(
        "srp,spd->srd",
        table,
        x.reshape(slabs, table.shape[2], -1),
        preferred_element_type=jnp.float32,
    )
    return out.reshape(x.shape)


def synth(table, x):
    slabs = table.shape[0]
    out = jnp.einsum(
        "srp,srd->spd",
        table,
        x.reshape(slabs, table.shape[1], -1),
        preferred_element_type=jnp.float32,
    )
    return out.reshape(x.shape)


def block_mix(real, imag, weight, bias):
    n = real.shape[0]
    part_re = real.reshape(n, BLOCKS, -1)
    part_im = imag.reshape(n, BLOCKS, -1)

    def prod(a, w):
        return jnp.einsum("nkc,kcd->nkd", a, w, preferred_element_type=jnp.float32)

    out_re = prod(part_re, weight[0]) - prod(part_im, weight[1])
    out_im = prod(part_re, weight[1]) + prod(part_im, weight[0])
    return (out_re.reshape(n, -1) + bias[0], out_im.reshape(n, -1) + bias[1])


def block_back(grad_re, grad_im, weight):
    n = grad_re.shape[0]
    part_re = grad_re.reshape(n, BLOCKS, -1)
    part_im = grad_im.reshape(n, BLOCKS, -1)

    def prod(g, w):
        return jnp.einsum("nkd,kcd->nkc", g, w, preferred_element_type=jnp.float32)

    in_re = prod(part_re, weight[0]) + prod(part_im, weight[1])
    in_im = prod(part_im, weight[0]) - prod(part_re, weight[1])
    return (in_re.reshape(n, -1), in_im.reshape(n, -1))


def block_outer(in_re, in_im, grad_re, grad_im):
    n = in_re.shape[0]
    left_re = in_re.reshape(n, BLOCKS, -1)
    left_im = in_im.reshape(n, BLOCKS, -1)
    right_re = grad_re.reshape(n, BLOCKS, -1)
    right_im = grad_im.reshape(n, BLOCKS, -1)

    def outer(a, g):
        return jnp.einsum("nkc,nkd->kcd", a, g, preferred_element_type=jnp.float32)

    weight_re = outer(left_re, right_re) + outer(left_im, right_im)
    weight_im = outer(left_re, right_im) - outer(left_im, right_re)
    return jnp.stack([weight_re, weight_im])


def split_sums(grad_re, grad_im):
    return jnp.stack(
        [jnp.sum(grad_re.astype(jnp.float32), 0), jnp.sum(grad_im.astype(jnp.float32), 0)]
    )


def send_modes(first, second):
    return (first, second)


def return_modes(first, second):
    return (first, second)


def send_grads(first, second):
    return (first, second)


def return_grads(first, second):
    return (first, second)


def layer_forward(hidden, weights, table_re, table_im):
    gain1, shift1, weight1, bias1, weight2, bias2, gain2, shift2, dense1, dbias1, dense2, dbias2 = (
        weights
    )
    u = layer_norm(hidden, gain1, shift1)
    u_low = u.astype(jnp.bfloat16)
    z_re = spectral(table_re, u_low).astype(jnp.bfloat16)
    z_im = spectral(table_im, u_low).astype(jnp.bfloat16)
    z_re, z_im = send_modes(z_re, z_im)
    a_re, a_im = block_mix(z_re, z_im, weight1, bias1)
    o_re = jax.nn.gelu(a_re).astype(jnp.bfloat16)
    o_im = jax.nn.gelu(a_im).astype(jnp.bfloat16)
    e_re, e_im = block_mix(o_re, o_im, weight2, bias2)
    s_re = shrink(e_re).astype(jnp.bfloat16)
    s_im = shrink(e_im).astype(jnp.bfloat16)
    s_re, s_im = return_modes(s_re, s_im)
    y_sum = synth(table_re, s_re) + synth(table_im, s_im)
    mid = hidden + y_sum + u
    v_low = layer_norm(mid, gain2, shift2).astype(jnp.bfloat16)
    pre = jnp.dot(v_low, dense1, preferred_element_type=jnp.float32) + dbias1
    act = jax.nn.gelu(pre).astype(jnp.bfloat16)
    result = mid + jnp.dot(act, dense2, preferred_element_type=jnp.float32) + dbias2
    kept = (hidden, z_re, z_im, a_re, a_im, o_re, o_im, e_re, e_im, mid, v_low, pre, act)
    return (result, kept)


def layer_backward(grad, kept, weights, table_re, table_im):
    gain1, shift1, weight1, bias1, weight2, bias2, gain2, shift2, dense1, dbias1, dense2, dbias2 = (
        weights
    )
    hidden, z_re, z_im, a_re, a_im, o_re, o_im, e_re, e_im, mid, v_low, pre, act = kept
    dbias2_grad = jnp.sum(grad, 0)
    grad_low = grad.astype(jnp.bfloat16)
    dense2_grad = jnp.einsum("nf,nd->fd", act, grad_low, preferred_element_type=jnp.float32)
    grad_act = jnp.einsum("nd,fd->nf", grad_low, dense2, preferred_element_type=jnp.float32)
    grad_pre = jax.vjp(jax.nn.gelu, pre)[1](grad_act)[0].astype(jnp.bfloat16)
    dbias1_grad = jnp.sum(grad_pre.astype(jnp.float32), 0)
    dense1_grad = jnp.einsum("nd,nf->df", v_low, grad_pre, preferred_element_type=jnp.float32)
    grad_v = jnp.einsum("nf,df->nd", grad_pre, dense1, preferred_element_type=jnp.float32)
    norm_pull = jax.vjp(layer_norm, mid, gain2, shift2)[1]
    grad_mid_ln, gain2_grad, shift2_grad = norm_pull(grad_v)
    grad_mid = grad + grad_mid_ln
    grad_y = grad_mid.astype(jnp.bfloat16)
    grad_s_re = spectral(table_re, grad_y).astype(jnp.bfloat16)
    grad_s_im = spectral(table_im, grad_y).astype(jnp.bfloat16)
    grad_s_re, grad_s_im = send_grads(grad_s_re, grad_s_im)
    grad_e_re = jax.vjp(shrink, e_re)[1](grad_s_re.astype(jnp.float32))[0].astype(jnp.bfloat16)
    grad_e_im = jax.vjp(shrink, e_im)[1](grad_s_im.astype(jnp.float32))[0].astype(jnp.bfloat16)
    bias2_grad = split_sums(grad_e_re, grad_e_im)
    weight2_grad = block_outer(o_re, o_im, grad_e_re, grad_e_im)
    grad_o_re, grad_o_im = block_back(grad_e_re, grad_e_im, weight2)
    grad_a_re = jax.vjp(jax.nn.gelu, a_re)[1](grad_o_re)[0].astype(jnp.bfloat16)
    grad_a_im = jax.vjp(jax.nn.gelu, a_im)[1](grad_o_im)[0].astype(jnp.bfloat16)
    bias1_grad = split_sums(grad_a_re, grad_a_im)
    weight1_grad = block_outer(z_re, z_im, grad_a_re, grad_a_im)
    grad_z_re, grad_z_im = block_back(grad_a_re, grad_a_im, weight1)
    grad_z_re, grad_z_im = return_grads(
        grad_z_re.astype(jnp.bfloat16), grad_z_im.astype(jnp.bfloat16)
    )
    grad_u = synth(table_re, grad_z_re) + synth(table_im, grad_z_im) + grad_mid
    first_pull = jax.vjp(layer_norm, hidden, gain1, shift1)[1]
    grad_hidden_ln, gain1_grad, shift1_grad = first_pull(grad_u)
    grad_hidden = grad_mid + grad_hidden_ln
    grads = (
        gain1_grad,
        shift1_grad,
        weight1_grad,
        bias1_grad,
        weight2_grad,
        bias2_grad,
        gain2_grad,
        shift2_grad,
        dense1_grad,
        dbias1_grad,
        dense2_grad,
        dbias2_grad,
    )
    return (grad_hidden, grads)


def sum_all(grads):
    return lax.psum(
        (
            grads[0],
            grads[1],
            grads[2],
            grads[3],
            grads[4],
            grads[5],
            grads[6],
            grads[7],
            grads[8],
            grads[9],
            grads[10],
            grads[11],
        ),
        ("dp", "modes"),
    )


def on_device(
    x_in,
    cotangent,
    block_grid,
    keep_modes,
    norm1_gain,
    norm1_bias,
    mix_w1,
    mix_b1,
    mix_w2,
    mix_b2,
    norm2_gain,
    norm2_bias,
    fc1,
    fc1_bias,
    fc2,
    fc2_bias,
):
    slabs = block_grid.shape[0] // NBLK
    slab_rows = x_in.shape[0] // slabs
    table_re, table_im = jax.vmap(partial(dft_tables, keep=keep_modes, slab_rows=slab_rows))(
        block_grid.reshape(slabs, NBLK)
    )
    stacks = (
        norm1_gain,
        norm1_bias,
        mix_w1,
        mix_b1,
        mix_w2,
        mix_b2,
        norm2_gain,
        norm2_bias,
        fc1,
        fc1_bias,
        fc2,
        fc2_bias,
    )
    hidden = x_in.astype(jnp.float32)
    saved = []
    for layer in range(LAYERS):
        weights = tuple((p[layer] for p in stacks))
        hidden, kept = layer_forward(hidden, weights, table_re, table_im)
        saved.append(kept)
    output = hidden.astype(jnp.bfloat16)
    grad = cotangent.astype(jnp.float32)
    layer_grads = [None] * LAYERS
    for layer in reversed(range(LAYERS)):
        weights = tuple((p[layer] for p in stacks))
        grad, grads = layer_backward(grad, saved[layer], weights, table_re, table_im)
        layer_grads[layer] = grads
    stacked = tuple(
        (jnp.stack([layer_grads[layer][index] for layer in range(LAYERS)]) for index in range(12))
    )
    stacked = sum_all(stacked)
    return (output, grad.astype(jnp.bfloat16)) + tuple(stacked)


def solution(mesh):
    in_specs = (
        P(("dp", "modes"), None),
        P(("dp", "modes"), None),
        P(("dp", "modes")),
        P(),
        P(),
        P(),
        P(),
        P(),
        P(),
        P(),
        P(),
        P(),
        P(),
        P(),
        P(),
        P(),
    )
    out_specs = (
        P(("dp", "modes"), None),
        P(("dp", "modes"), None),
        P(),
        P(),
        P(),
        P(),
        P(),
        P(),
        P(),
        P(),
        P(),
        P(),
        P(),
        P(),
    )
    return jax.shard_map(
        on_device, mesh=mesh, in_specs=in_specs, out_specs=out_specs, check_vma=False
    )
```

profile of v0, /device:TPU:0, one launch (start us, length us, event | category | flops | bytes accessed | tf_op | source)
XLA Modules:
  0.0 1187.0 jit_solution(7400295041662060526)
XLA Ops:
  9.6 2.2 fusion.317
  11.8 58.0 %fusion.460 = bf16[1024,1024,1]{1,0,2:T(8,128)(2,1)S(1)} fusion(f32[1024]{0:T(1024)S(1)} %get-tuple-element.99, pred[1024]{0:T(1024)(128)(4,1)S(1)} %get-tuple-element.96, s32[1024]{0:T(1024)S(1)} %get-tuple-element.100, s32[1024]{0:T(1024)S(1)} %get-tuple-element.98, s32[1024]{0:T(1024)S(1)} %get-tuple-element.97, ...), kind=kLoop, calls=%fused_computation.218.clone.clone.clone.1 | loop fusion | flops 19922944 | bytes 2119680 | tf_op jit(solution)/shard_map/srp,spd->srd/dot_general | solution.py:51
  69.8 58.9 %fusion.462 = bf16[1024,1024,1]{1,0,2:T(8,128)(2,1)} fusion(f32[1024]{0:T(1024)S(1)} %get-tuple-element.99, pred[1024]{0:T(1024)(128)(4,1)S(1)} %get-tuple-element.96, s32[1024]{0:T(1024)S(1)} %get-tuple-element.100, s32[1024]{0:T(1024)S(1)} %get-tuple-element.98, s32[1024]{0:T(1024)S(1)} %get-tuple-element.97, ...), kind=kLoop, calls=%fused_computation.216.clone.clone.clone | loop fusion | flops 19922944 | bytes 2119680 | tf_op jit(solution)/shard_map/srp,spd->srd/dot_general | solution.py:51
  128.7 58.6 %fusion.456 = bf16[1024,1024,1]{1,0,2:T(8,128)(2,1)} fusion(f32[1024]{0:T(1024)S(1)} %get-tuple-element.99, pred[1024]{0:T(1024)(128)(4,1)S(1)} %get-tuple-element.96, s32[1024]{0:T(1024)S(1)} %get-tuple-element.100, s32[1024]{0:T(1024)S(1)} %get-tuple-element.98, s32[1024]{0:T(1024)S(1)} %get-tuple-element.97, ...), kind=kLoop, calls=%fused_computation.222.clone.clone.clone.1 | loop fusion | flops 18874368 | bytes 2119680 | tf_op jit(solution)/shard_map/srp,spd->srd/dot_general | solution.py:51
  188.1 1.9 copy.67
  194.6 2.4 fusion.147
  202.5 58.6 %fusion.458 = bf16[1024,1024,1]{1,0,2:T(8,128)(2,1)} fusion(f32[1024]{0:T(1024)S(1)} %get-tuple-element.99, pred[1024]{0:T(1024)(128)(4,1)S(1)} %get-tuple-element.96, s32[1024]{0:T(1024)S(1)} %get-tuple-element.100, s32[1024]{0:T(1024)S(1)} %get-tuple-element.98, s32[1024]{0:T(1024)S(1)} %get-tuple-element.97, ...), kind=kLoop, calls=%fused_computation.220.clone.clone.clone | loop fusion | flops 18874368 | bytes 2119680 | tf_op jit(solution)/shard_map/srp,spd->srd/dot_general | solution.py:51
  261.1 58.9 %select_convert_fusion.7.clone.4 = bf16[1024,1024]{1,0:T(8,128)(2,1)} fusion(f32[1024]{0:T(1024)S(1)} %get-tuple-element.99, s32[1024]{0:T(1024)S(1)} %get-tuple-element.101, pred[1024]{0:T(1024)(128)(4,1)S(1)} %get-tuple-element.96, s32[1024]{0:T(1024)S(1)} %get-tuple-element.100, s32[1024]{0:T(1024)S(1)} %get-tuple-element.98, ...), kind=kLoop, calls=%fused_computation.8.clone.1.clone.clone.clone.1 | loop fusion | flops 19922944 | bytes 2119680 | tf_op jit(solution)/shard_map/reduce_sum | solution.py:114
  320.0 58.7 %select_convert_fusion.5.clone.4 = bf16[1024,1024]{1,0:T(8,128)(2,1)} fusion(f32[1024]{0:T(1024)S(1)} %get-tuple-element.99, s32[1024]{0:T(1024)S(1)} %get-tuple-element.101, pred[1024]{0:T(1024)(128)(4,1)S(1)} %get-tuple-element.96, s32[1024]{0:T(1024)S(1)} %get-tuple-element.100, s32[1024]{0:T(1024)S(1)} %get-tuple-element.98, ...), kind=kLoop, calls=%fused_computation.9.clone.1.clone.clone.clone.1 | loop fusion | flops 18874368 | bytes 2119680 | tf_op jit(solution)/shard_map/reduce_sum | solution.py:114
  379.6 4.3 fusion.146
  383.9 2.2 fusion.33
  386.2 68.7 %fusion.150 = f32[1024,512]{0,1:T(8,128)S(1)} fusion(bf16[1024,512]{0,1:T(8,128)(2,1)S(1)} %bitcast.595, f32[1024]{0:T(1024)S(1)} %get-tuple-element.99, s32[1024]{0:T(1024)S(1)} %get-tuple-element.101, pred[1024]{0:T(1024)(128)(4,1)S(1)} %get-tuple-element.96, s32[1024]{0:T(1024)S(1)} %get-tuple-element.100, s32[1024]{0:T(1024)S(1)} %get-tuple-element.98, ...), kind=kOutput, calls=%fused_computation.231 | convolution fusion | flops 1093664768 | bytes 3168256 | tf_op jit(solution)/shard_map/srp,srd->spd/dot_general | solution.py:62
  454.9 2.2 fusion.25
  457.2 58.7 %fusion.347 = (f32[1024]{0:T(1024)S(1)}, f32[1024,512]{0,1:T(8,128)S(1)}) fusion(f32[512]{0:T(512)S(1)} %bitcast.629, f32[512]{0:T(512)S(1)} %bitcast.610, f32[1024]{0:T(1024)S(1)} %fusion.318, f32[1024]{0:T(1024)S(1)} %broadcast_multiply_fusion.3, f32[1024,512]{0,1:T(8,128)S(1)} %fusion.150, bf16[1024,512]{0,1:T(8,128)(2,1)S(1)} %bitcast.593, ...), kind=kOutput, calls=%fused_computation.533 | convolution fusion | flops 1097333760 | bytes 6330368 | tf_op jit(solution)/shard_map/srp,srd->spd/dot_general | solution.py:62
  526.1 2.5 fusion.137
  534.2 2.3 copy.77
  536.5 4.5 fusion.136
  541.0 2.2 fusion.49
  543.2 58.1 %fusion.154 = f32[1024,512]{0,1:T(8,128)S(1)} fusion(bf16[1024,512]{0,1:T(8,128)(2,1)S(1)} %bitcast.596, f32[1024]{0:T(1024)S(1)} %get-tuple-element.99, s32[1024]{0:T(1024)S(1)} %get-tuple-element.101, pred[1024]{0:T(1024)(128)(4,1)S(1)} %get-tuple-element.96, s32[1024]{0:T(1024)S(1)} %get-tuple-element.100, s32[1024]{0:T(1024)S(1)} %get-tuple-element.98, ...), kind=kOutput, calls=%fused_computation.235 | convolution fusion | flops 1093664768 | bytes 3168256 | tf_op jit(solution)/shard_map/srp,srd->spd/dot_general | solution.py:62
  601.3 2.2 fusion.41
  603.5 58.6 %fusion.349 = (f32[1024]{0:T(1024)S(1)}, f32[1024,512]{0,1:T(8,128)S(1)}) fusion(f32[512]{0:T(512)S(1)} %bitcast.626, f32[512]{0:T(512)S(1)} %bitcast.600, f32[1024]{0:T(1024)S(1)} %fusion.320, f32[1024,512]{0,1:T(8,128)S(1)} %copy-done.4, f32[1024]{0:T(1024)S(1)} %broadcast_multiply_fusion.1, f32[1024,512]{0,1:T(8,128)S(1)} %fusion.154, ...), kind=kOutput, calls=%fused_computation.535 | convolution fusion | flops 1096809472 | bytes 7378944 | tf_op jit(solution)/shard_map/srp,srd->spd/dot_general | solution.py:62
  665.4 2.1 convolution_bitcast_fusion
  667.5 2.5 convert_reduce_fusion.2
  671.8 2.7 fusion.350
  674.5 3.1 copy.78
  677.6 3.6 multiply_reduce_fusion
  684.7 2.9 convert_reduce_fusion.4
  692.2 2.9 convert_reduce_fusion.5
  699.3 2.4 convert_reduce_fusion.9
  704.4 2.4 convert_reduce_fusion.8
  709.3 58.0 %fusion.148 = f32[1024,512]{0,1:T(8,128)S(1)} fusion(bf16[1024,512]{0,1:T(8,128)(2,1)S(1)} %bitcast.598, f32[1024]{0:T(1024)S(1)} %get-tuple-element.99, s32[1024]{0:T(1024)S(1)} %get-tuple-element.101, pred[1024]{0:T(1024)(128)(4,1)S(1)} %get-tuple-element.96, s32[1024]{0:T(1024)S(1)} %get-tuple-element.100, s32[1024]{0:T(1024)S(1)} %get-tuple-element.98, ...), kind=kOutput, calls=%fused_computation.229 | convolution fusion | flops 1093664768 | bytes 3168256 | tf_op jit(solution)/shard_map/srp,srd->spd/dot_general | solution.py:62
  767.3 58.9 %fusion.337 = (f32[512]{0:T(512)S(1)}, f32[1024]{0:T(1024)S(1)}, f32[1024,512]{0,1:T(8,128)S(1)}) fusion(f32[512]{0:T(512)S(1)} %bitcast.601, f32[1024,512]{0,1:T(8,128)S(1)} %copy-done.5, f32[1024]{0:T(1024)S(1)} %broadcast_multiply_fusion.1, f32[1024,512]{0,1:T(8,128)S(1)} %get-tuple-element.77, f32[1024]{0:T(1024)S(1)} %negate_multiply_fusion.3, ...), kind=kOutput, calls=%fused_computation.523 | convolution fusion | flops 1097857536 | bytes 10524672 | tf_op jit(solution)/shard_map/srp,srd->spd/dot_general | solution.py:62
  828.8 2.2 convolution_bitcast_fusion.1
  830.9 2.1 convert_reduce_fusion.3
  834.8 2.1 fusion.351
  837.0 2.9 copy.89
  839.9 2.1 multiply_reduce_fusion.3
  843.7 2.2 add_add_fusion.13
  847.7 60.6 %convert_reduce_fusion.6 = (f32[512]{0:T(512)S(1)}, f32[1024,512]{0,1:T(8,128)S(1)}) fusion(f32[512]{0:T(512)S(1)} %bitcast.631, f32[8,1024,64]{1,2,0:T(8,128)S(1)} %copy-done.43, f32[1024]{0:T(1024)S(1)} %get-tuple-element.99, s32[1024]{0:T(1024)S(1)} %get-tuple-element.101, pred[1024]{0:T(1024)(128)(4,1)S(1)} %get-tuple-element.96, ...), kind=kOutput, calls=%fused_computation.251 | convolution fusion | flops 1104150016 | bytes 5269504 | tf_op jit(solution)/shard_map/srp,spd->srd/dot_general | solution.py:51
  912.3 59.9 %convert_reduce_fusion.7 = (f32[512]{0:T(512)S(1)}, f32[1024,512]{0,1:T(8,128)S(1)}) fusion(f32[512]{0:T(512)S(1)} %bitcast.630, f32[8,1024,64]{1,2,0:T(8,128)S(1)} %copy-done.42, f32[1024]{0:T(1024)S(1)} %get-tuple-element.99, s32[1024]{0:T(1024)S(1)} %get-tuple-element.101, pred[1024]{0:T(1024)(128)(4,1)S(1)} %get-tuple-element.96, ...), kind=kOutput, calls=%fused_computation.252 | convolution fusion | flops 1103101440 | bytes 5269504 | tf_op jit(solution)/shard_map/srp,spd->srd/dot_general | solution.py:51
  999.3 58.1 %fusion.152 = f32[1024,512]{0,1:T(8,128)S(1)} fusion(bf16[1024,512]{0,1:T(8,128)(2,1)S(1)} %bitcast.597, f32[1024]{0:T(1024)S(1)} %get-tuple-element.99, s32[1024]{0:T(1024)S(1)} %get-tuple-element.101, pred[1024]{0:T(1024)(128)(4,1)S(1)} %get-tuple-element.96, s32[1024]{0:T(1024)S(1)} %get-tuple-element.100, s32[1024]{0:T(1024)S(1)} %get-tuple-element.98, ...), kind=kOutput, calls=%fused_computation.233 | convolution fusion | flops 1093664768 | bytes 3168256 | tf_op jit(solution)/shard_map/srp,srd->spd/dot_general | solution.py:62
  1057.4 59.7 %fusion.336 = (f32[512]{0:T(512)S(1)}, f32[1024]{0:T(1024)S(1)}, f32[1024,512]{0,1:T(8,128)}) fusion(f32[512]{0:T(512)S(1)} %bitcast.611, f32[1024]{0:T(1024)S(1)} %copy-done.79, bf16[1024,512]{0,1:T(8,128)(2,1)S(1)} %copy-done.1, f32[1024,512]{0,1:T(8,128)S(1)} %add_add_fusion.13, f32[1024,512]{0,1:T(8,128)S(1)} %fusion.152, ...), kind=kOutput, calls=%fused_computation.522 | convolution fusion | flops 1096808960 | bytes 8423424 | tf_op jit(solution)/shard_map/srp,srd->spd/dot_general | solution.py:62
  1117.3 2.1 add_convert_fusion.3
  1119.4 2.4 copy.102
  1122.1 2.8 fusion.23
  1126.6 2.3 copy.103
  1129.1 43.7 %all-reduce = (f32[2,512]{1,0:T(2,128)}, f32[2,512]{1,0:T(2,128)}, f32[2,2,512]{2,1,0:T(2,128)}, f32[2,2,512]{2,1,0:T(2,128)}, f32[2,512]{1,0:T(2,128)}, /*index...) all-reduce(f32[2,512]{1,0:T(2,128)S(1)} %pad_maximum_fusion.6, ...), channel_id=1, replica_groups=mesh['dp'=2,'modes'=16] {'dp','modes'}, use_global_device_ids=true, to_apply=%region_19.20 | all-reduce | flops 10240 | bytes 81920 | tf_op jit(solution)/shard_map/psum | solution.py:215
  1172.8 2.5 copy.137
  (367 shorter events, 97.2 us)
Async XLA Ops:
  7.2 1165.6 %all-reduce.4.cloned.1.call-start = ((), (), s32[]{:S(2)}) async-start(), calls=%async_computation | async-start | bytes 12582912 | tf_op jit(solution)/shard_map/psum | solution.py:215
  69.8 117.6 %copy-start.96 = (f32[2,512]{1,0:T(2,128)S(1)}, f32[2,512]{1,0:T(2,128)}, u32[]{:S(2)}) copy-start(f32[2,512]{1,0:T(2,128)} %param.20) | copy-start | bytes 12292
  69.8 117.6 %copy-start.97 = (f32[2,512]{1,0:T(2,128)S(1)}, f32[2,512]{1,0:T(2,128)}, u32[]{:S(2)}) copy-start(f32[2,512]{1,0:T(2,128)} %param.21) | copy-start | bytes 12292
  69.8 117.6 %copy-start.92 = (f32[2,2,512]{2,1,0:T(2,128)S(1)}, f32[2,2,512]{2,1,0:T(2,128)}, u32[]{:S(2)}) copy-start(f32[2,2,512]{2,1,0:T(2,128)} %param.23) | copy-start | bytes 24580
  69.8 117.6 %copy-start.93 = (f32[2,2,512]{2,1,0:T(2,128)S(1)}, f32[2,2,512]{2,1,0:T(2,128)}, u32[]{:S(2)}) copy-start(f32[2,2,512]{2,1,0:T(2,128)} %param.25) | copy-start | bytes 24580
  187.4 269.8 %copy-start.88 = (f32[1,512]{1,0:T(1,128)}, f32[1,512]{1,0:T(1,128)S(1)}, u32[]{:S(2)}) copy-start(f32[1,512]{1,0:T(1,128)S(1)} %get-tuple-element.92) | copy-start | bytes 6148
  190.1 267.1 %copy-start = (bf16[1024,512]{0,1:T(8,128)(2,1)}, bf16[1024,512]{0,1:T(8,128)(2,1)S(1)}, u32[]{:S(2)}) copy-start(bf16[1024,512]{0,1:T(8,128)(2,1)S(1)} %copy.67) | copy-start | bytes 3145732
  190.3 266.9 %copy-start.78 = (f32[1024]{0:T(1024)}, f32[1024]{0:T(1024)S(1)}, u32[]{:S(2)}) copy-start(f32[1024]{0:T(1024)S(1)} %broadcast_multiply_fusion.3) | copy-start | bytes 12292
  190.6 266.5 %copy-start.80 = (f32[1024]{0:T(1024)}, f32[1024]{0:T(1024)S(1)}, u32[]{:S(2)}) copy-start(f32[1024]{0:T(1024)S(1)} %fusion.318) | copy-start | bytes 12292
  194.0 6.6 copy-start.17
  197.0 3.6 copy-start.7
  261.0 117.6 %copy-start.98 = (f32[2,512]{1,0:T(2,128)S(1)}, f32[2,512]{1,0:T(2,128)}, u32[]{:S(2)}) copy-start(f32[2,512]{1,0:T(2,128)} %param.26) | copy-start | bytes 12292
  261.0 117.6 %copy-start.99 = (f32[2,512]{1,0:T(2,128)S(1)}, f32[2,512]{1,0:T(2,128)}, u32[]{:S(2)}) copy-start(f32[2,512]{1,0:T(2,128)} %param.27) | copy-start | bytes 12292
  261.0 117.7 %copy-start.100 = (f32[2,512]{1,0:T(2,128)S(1)}, f32[2,512]{1,0:T(2,128)}, u32[]{:S(2)}) copy-start(f32[2,512]{1,0:T(2,128)} %param.29) | copy-start | bytes 12292
  261.0 117.7 %copy-start.101 = (f32[2,512]{1,0:T(2,128)S(1)}, f32[2,512]{1,0:T(2,128)}, u32[]{:S(2)}) copy-start(f32[2,512]{1,0:T(2,128)} %param.31) | copy-start | bytes 12292
  261.1 118.6 %copy-start.30 = (bf16[1024,8,64]{0,2,1:T(8,128)(2,1)S(1)}, bf16[1024,8,64]{0,2,1:T(8,128)(2,1)}, u32[]{:S(2)}) copy-start(bf16[1024,8,64]{0,2,1:T(8,128)(2,1)} %copy-done.29) | copy-start | bytes 3145732
  378.7 288.7 %copy-start.104 = (f32[1,512]{1,0:T(1,128)}, f32[1,512]{1,0:T(1,128)S(1)}, u32[]{:S(2)}) copy-start(f32[1,512]{1,0:T(1,128)S(1)} %get-tuple-element.83) | copy-start | bytes 6148
  379.4 4.5 copy-start.86
  379.5 75.4 %copy-start.84 = (f32[8,64]{1,0:T(8,128)}, f32[8,64]{1,0:T(8,128)S(1)}, u32[]{:S(2)}) copy-start(f32[8,64]{1,0:T(8,128)S(1)} %add.786) | copy-start | bytes 6148
  379.6 4.3 copy-start.47
  379.6 4.3 copy-start.51
  383.9 71.0 %copy-start.9 = (bf16[1024,8,64]{0,2,1:T(8,128)(2,1)}, bf16[1024,8,64]{0,2,1:T(8,128)(2,1)S(1)}, u32[]{:S(2)}) copy-start(bf16[1024,8,64]{0,2,1:T(8,128)(2,1)S(1)} %get-tuple-element.107) | copy-start | bytes 3145732
  386.2 68.7 %copy-start.46 = (f32[8,1024,64]{1,2,0:T(8,128)S(1)}, f32[8,1024,64]{1,2,0:T(8,128)}, u32[]{:S(2)}) copy-start(f32[8,1024,64]{1,2,0:T(8,128)} %fusion.263) | copy-start | bytes 6291460
  515.9 326.1 %copy-start.2 = (f32[1024,512]{0,1:T(8,128)}, f32[1024,512]{0,1:T(8,128)S(1)}, u32[]{:S(2)}) copy-start(f32[1024,512]{0,1:T(8,128)S(1)} %get-tuple-element.114) | copy-start | bytes 6291460
  525.6 6.6 copy-start.19
  536.5 4.5 copy-start.49
  536.5 4.5 copy-start.52
  541.0 60.3 %copy-start.11 = (bf16[1024,8,64]{0,2,1:T(8,128)(2,1)}, bf16[1024,8,64]{0,2,1:T(8,128)(2,1)S(1)}, u32[]{:S(2)}) copy-start(bf16[1024,8,64]{0,2,1:T(8,128)(2,1)S(1)} %get-tuple-element.119) | copy-start | bytes 3145732
  543.2 58.1 %copy-start.48 = (f32[8,1024,64]{1,2,0:T(8,128)S(1)}, f32[8,1024,64]{1,2,0:T(8,128)}, u32[]{:S(2)}) copy-start(f32[8,1024,64]{1,2,0:T(8,128)} %fusion.239) | copy-start | bytes 6291460
  662.2 7.9 copy-start.13
  677.6 3.6 copy-start.14
  677.6 3.6 copy-start.16
  689.0 9.1 copy-start.21
  696.5 6.7 copy-start.23
  709.3 58.0 %copy-start.5 = (f32[1024,512]{0,1:T(8,128)S(1)}, f32[1024,512]{0,1:T(8,128)}, u32[]{:S(2)}) copy-start(f32[1024,512]{0,1:T(8,128)} %copy-done.3) | copy-start | bytes 6291460
  847.7 60.6 %copy-start.87 = (f32[8,64]{1,0:T(8,128)S(1)}, f32[8,64]{1,0:T(8,128)}, u32[]{:S(2)}) copy-start(f32[8,64]{1,0:T(8,128)} %copy-done.86) | copy-start | bytes 6148
  912.3 59.9 %copy-start.85 = (f32[8,64]{1,0:T(8,128)S(1)}, f32[8,64]{1,0:T(8,128)}, u32[]{:S(2)}) copy-start(f32[8,64]{1,0:T(8,128)} %copy-done.84) | copy-start | bytes 6148
  999.2 58.1 %copy-start.1 = (bf16[1024,512]{0,1:T(8,128)(2,1)S(1)}, bf16[1024,512]{0,1:T(8,128)(2,1)}, u32[]{:S(2)}) copy-start(bf16[1024,512]{0,1:T(8,128)(2,1)} %copy-done) | copy-start | bytes 3145732
  999.2 58.1 %copy-start.79 = (f32[1024]{0:T(1024)S(1)}, f32[1024]{0:T(1024)}, u32[]{:S(2)}) copy-start(f32[1024]{0:T(1024)} %copy-done.78) | copy-start | bytes 12292
  999.3 58.1 %copy-start.89 = (f32[1,512]{1,0:T(1,128)S(1)}, f32[1,512]{1,0:T(1,128)}, u32[]{:S(2)}) copy-start(f32[1,512]{1,0:T(1,128)} %copy-done.88) | copy-start | bytes 6148
  1057.4 59.8 %copy-start.15 = (f32[1024,512]{0,1:T(8,128)S(1)}, f32[1024,512]{0,1:T(8,128)}, u32[]{:S(2)}) copy-start(f32[1024,512]{0,1:T(8,128)} %copy-done.13) | copy-start | bytes 6291460
  1057.4 59.8 %copy-start.105 = (f32[1,512]{1,0:T(1,128)S(1)}, f32[1,512]{1,0:T(1,128)}, u32[]{:S(2)}) copy-start(f32[1,512]{1,0:T(1,128)} %copy-done.104) | copy-start | bytes 6148
  1057.4 59.8 %copy-start.106 = (f32[1,512]{1,0:T(1,128)S(1)}, f32[1,512]{1,0:T(1,128)}, u32[]{:S(2)}) copy-start(f32[1,512]{1,0:T(1,128)} %get-tuple-element.89) | copy-start | bytes 6148
  1057.4 59.8 %copy-start.113 = (bf16[2,512,512]{2,1,0:T(8,128)(2,1)S(1)}, bf16[2,512,512]{2,1,0:T(8,128)(2,1)}, u32[]{:S(2)}) copy-start(bf16[2,512,512]{2,1,0:T(8,128)(2,1)} %param.30) | copy-start | bytes 3145732
  1057.4 59.8 %copy-start.115 = (f32[1024,512]{1,0:T(8,128)S(1)}, f32[1024,512]{1,0:T(8,128)}, u32[]{:S(2)}) copy-start(f32[1024,512]{1,0:T(8,128)} %copy-done.114) | copy-start | bytes 6291460
  1119.4 2.7 copy-start.81
  1122.1 2.8 copy-start.39
  1172.8 3.4 copy-start.61
  (71 other events, 127.0 us)
Sparse Core Ops, SparseCore 0:
  995.5 160.1 all-reduce.3
where the time goes:
time: 1190 us
  matrix products  691 us (58%)
  other arithmetic  385 us (32%)
  local copies, waits for them, and re-layouts  51.6 us (4%)
  blocking collectives  43.7 us (4%)
  between operations  15.8 us (1%)
    dot_general x8, matrix products, synth(): jnp.einsum('srp,srd->spd', table, x.reshape(slabs, table.shape[1], -1), p...  479 us
    dot_general x4, other arithmetic, spectral(): jnp.einsum('srp,spd->srd', table, x.reshape(slabs, table.shape[2], -1), p...  234 us
    dot_general x8, matrix products, spectral(): jnp.einsum('srp,spd->srd', table, x.reshape(slabs, table.shape[2], -1), p...  131 us
    reduce_sum x2, other arithmetic, split_sums(): jnp.sum(grad_im.astype(jnp.float32), 0)  59 us
    reduce_sum x2, other arithmetic, split_sums(): jnp.sum(grad_re.astype(jnp.float32), 0)  58.9 us
    psum x1, blocking collectives, sum_all(): lax.psum((grads[0], grads[1], grads[2], grads[3], grads[4], grads[5], gra...  43.7 us
    unnamed x244, local copies, waits for them, and re-layouts  42.1 us
    dot_general x16, matrix products, prod(): return jnp.einsum('nkc,kcd->nkd', a, w, preferred_element_type=jnp.float32)  34.5 us
  transfers between devices with their start and end apart: 1, of which 0 were waited for; matrix products, arithmetic and copies ran while one was open for 11% of the time, Pallas kernels for 0%

commit v1 on v0

v1 whole, which is shorter than its diff:
```python
import math
from functools import partial

import jax
import jax.numpy as jnp
from jax import lax
from jax.experimental import pallas as pl
from jax.experimental.pallas import tpu as pltpu
from jax.sharding import PartitionSpec as P

LAYERS = 2
NBLK = 16
F32 = jnp.float32
BF = jnp.bfloat16
C0 = math.sqrt(2.0 / math.pi)
C1 = 0.044715 * C0
PER = 1296
RT = 256
CH = 64


def nn(a, b):
    return jnp.dot(a, b, preferred_element_type=F32)


def nt(a, b):
    return lax.dot_general(a, b, (((1,), (1,)), ((), ())), preferred_element_type=F32)


def tn(a, b):
    return lax.dot_general(a, b, (((0,), (0,)), ((), ())), preferred_element_type=F32)


def gelu_pair(x):
    x2 = x * x
    p = 0.5 + 0.5 * jnp.tanh(x * (C0 + C1 * x2))
    y = x * p
    return y, p + y * (1.0 - p) * (2.0 * C0 + (6.0 * C1) * x2)


def cos_sin(t):
    x = t - 0.5
    w = (2.0 * math.pi * x) ** 2
    c = jnp.full_like(w, 1.0 / math.factorial(16))
    s = jnp.full_like(w, -1.0 / math.factorial(15))
    for k in range(7, -1, -1):
        c = c * w + (-1.0) ** k / math.factorial(2 * k)
        if k < 7:
            s = s * w + (-1.0) ** k / math.factorial(2 * k + 1)
    return -c, -s * (2.0 * math.pi * x)


def pick(values, block):
    out = jnp.zeros(block.shape, jnp.int32)
    for j in range(NBLK):
        out = jnp.where(block == j, values[j], out)
    return out


def split(index, grid):
    span = grid * grid
    start = index & ~(span - 1)
    local = index & (span - 1)
    lg = jnp.where(grid == 8, 3, jnp.where(grid == 16, 4, 5))
    return start, lax.shift_right_logical(local, lg), local & (grid - 1)


def build_tables(grid_ref, keep_ref, cre, cim, m1, m2, m3):
    rows = cre.shape[0]
    unit = rows // NBLK
    vals = [grid_ref[j] for j in range(NBLK)]
    keep = [keep_ref[j] for j in range(3)]
    lane = lax.broadcasted_iota(jnp.int32, (8, rows), 1)
    gc = pick(vals, lane // unit)
    start_c, p_c, q_c = split(lane, gc)
    ginv = 1.0 / gc.astype(F32)
    sub = lax.broadcasted_iota(jnp.int32, (8, rows), 0)
    bcs = []
    for j in range(4):
        q_r = (sub + 8 * j) & (gc - 1)
        t = ((q_r * q_c) & (gc - 1)).astype(F32) * ginv
        bcs.append(cos_sin(t))

    def step(i, carry):
        blk = sub + 8 * i
        r = blk * 8
        gb = jnp.full((8, rows), 0, jnp.int32) + grid_ref[(64 * i) // unit]
        start_b, p_b, _ = split(r, gb)
        t = ((p_b * p_c) & (gc - 1)).astype(F32) * ginv
        ac, as_ = cos_sin(t)
        same = jnp.where(start_b == start_c, ginv, 0.0)
        ac = ac * same
        as_ = as_ * same
        for j in range(8):
            bc, bs = bcs[j % 4]
            a1 = ac[j : j + 1, :]
            a2 = as_[j : j + 1, :]
            if j % 2 == 0:
                bc2, bs2 = bcs[(j + 1) % 4]
                b1 = ac[j + 1 : j + 2, :]
                b2 = as_[j + 1 : j + 2, :]
                re = jnp.concatenate([a1 * bc - a2 * bs, b1 * bc2 - b2 * bs2], 0)
                im = jnp.concatenate([-(a2 * bc + a1 * bs), -(b2 * bc2 + b1 * bs2)], 0)
                dst = pl.ds(pl.multiple_of(i * 64 + j * 8, 16), 16)
                cre[dst, :] = re.astype(BF)
                cim[dst, :] = im.astype(BF)
        return carry

    lax.fori_loop(0, rows // 64, step, 0)

    def mask(i, carry):
        r = lax.broadcasted_iota(jnp.int32, (64, 128), 0) + 64 * i
        gb = jnp.full((64, 128), 0, jnp.int32) + grid_ref[(64 * i) // unit]
        _, p, q = split(r, gb)
        k = jnp.where(gb == 8, keep[0], jnp.where(gb == 16, keep[1], keep[2]))
        m = jnp.where((p < k) & (q < k), 1.0, 0.0)
        dst = pl.ds(pl.multiple_of(i * 64, 64), 64)
        m1[dst, :] = m
        m2[dst, :] = m * 0.05
        m3[dst, :] = m * (0.05 * 0.0025)
        return carry

    lax.fori_loop(0, rows // 64, mask, 0)


def build_mix(w_ref, out_ref):
    i = lax.broadcasted_iota(jnp.int32, (64, 128), 0)
    j = lax.broadcasted_iota(jnp.int32, (64, 128), 1)
    dup = jnp.where((j & 63) == i, 1.0, 0.0).astype(BF)
    r = lax.broadcasted_iota(jnp.int32, (512, 128), 0)
    c = lax.broadcasted_iota(jnp.int32, (512, 128), 1)
    diag = ((r // 64) & 1) == (c // 64)
    for layer in range(LAYERS):
        re = jnp.where(diag, nn(w_ref[layer, 0], dup), 0.0)
        im = jnp.where(diag, nn(w_ref[layer, 1], dup), 0.0)
        for g in range(4):
            a = re[g * 128 : (g + 1) * 128].astype(BF)
            b = im[g * 128 : (g + 1) * 128]
            out_ref[layer, g, 0:128, 0:128] = a
            out_ref[layer, g, 128:256, 128:256] = a
            out_ref[layer, g, 0:128, 128:256] = b.astype(BF)
            out_ref[layer, g, 128:256, 0:128] = (-b).astype(BF)


def fold(x):
    return jnp.sum(x.reshape(x.shape[0] // 8, 8, x.shape[1]), 0)


def kernel(
    grid_ref, keep_ref, x_ref, cot_ref,
    n1g, n1b, w1, b1, w2, b2, n2g, n2b, fc1, fb1, fc2, fb2,
    out_ref, xg_ref, grads_ref,
    cre, cim, m1, m2, m3, w1g, w2g,
    xh1, rs1, hu, ul, z, o, da, ds, sr, si, xh2, rs2, v, act, dp,
    gm, gmid, acc,
):
    g_s, gy, gzr, gzi = hu, ul, sr, si
    rows = x_ref.shape[0]
    tiles = rows // RT
    build_tables(grid_ref, keep_ref, cre, cim, m1, m2, m3)
    build_mix(w1, w1g)
    build_mix(w2, w2g)
    acc[...] = jnp.zeros_like(acc)

    def tile(i):
        return pl.ds(pl.multiple_of(i * RT, RT), RT)

    def chunk(i, j):
        return pl.ds(pl.multiple_of(i * RT + j * CH, CH), CH)

    def add_to(layer, k, x):
        acc[layer, k] = acc[layer, k] + fold(x)

    def norm1(layer, dst, h):
        mean = jnp.mean(h, -1, keepdims=True)
        cent = h - mean
        rstd = lax.rsqrt(jnp.mean(cent * cent, -1, keepdims=True) + 1e-05)
        xh = cent * rstd
        u = xh * n1g[layer : layer + 1, :] + n1b[layer : layer + 1, :]
        xh1[layer, dst, :] = xh
        rs1[layer, dst, :] = jnp.broadcast_to(rstd, (CH, 128))
        ul[dst, :] = u.astype(BF)
        hu[dst, :] = h + u

    def enter(i, carry):
        for j in range(RT // CH):
            dst = chunk(i, j)
            norm1(0, dst, x_ref[dst, :].astype(F32))
        return carry

    lax.fori_loop(0, tiles, enter, 0)

    def mix_forward(layer):
        def body(i, carry):
            dst = tile(i)
            zr = nn(cre[dst, :], ul[...]).astype(BF)
            zi = nn(cim[dst, :], ul[...]).astype(BF)
            k1 = jnp.concatenate([m1[dst, :]] * 2, 1)
            k2 = jnp.concatenate([m2[dst, :]] * 2, 1)
            k3 = jnp.concatenate([m3[dst, :]] * 2, 1)
            for g in range(4):
                sl = slice(g * 128, (g + 1) * 128)
                gl = slice(g * 256, (g + 1) * 256)
                zg = jnp.concatenate([zr[:, sl], zi[:, sl]], 1)
                z[layer, dst, gl] = zg
                bias1 = jnp.concatenate([b1[layer, 0:1, sl], b1[layer, 1:2, sl]], 1)
                a = nn(zg, w1g[layer, g]) + bias1
                og, dag = gelu_pair(a)
                og = og.astype(BF)
                o[layer, dst, gl] = og
                da[layer, dst, gl] = dag.astype(BF)
                bias2 = jnp.concatenate([b2[layer, 0:1, sl], b2[layer, 1:2, sl]], 1)
                e = nn(og, w2g[layer, g]) + bias2
                r = lax.rsqrt(e * e + 0.0025)
                s = e * (k1 - k2 * r)
                ds[layer, dst, gl] = (k1 - k3 * (r * r * r)).astype(BF)
                sr[dst, sl] = s[:, 0:128].astype(BF)
                si[dst, sl] = s[:, 128:256].astype(BF)
            return carry

        lax.fori_loop(0, tiles, body, 0)

    def ff_forward(layer):
        def body(i, carry):
            dst = tile(i)
            y = nn(cre[dst, :], sr[...]) + nn(cim[dst, :], si[...])
            mids = []
            for j in range(RT // CH):
                cd = chunk(i, j)
                mid = y[j * CH : (j + 1) * CH] + hu[cd, :]
                mean = jnp.mean(mid, -1, keepdims=True)
                cent = mid - mean
                rstd = lax.rsqrt(jnp.mean(cent * cent, -1, keepdims=True) + 1e-05)
                xh = cent * rstd
                xh2[layer, cd, :] = xh
                rs2[layer, cd, :] = jnp.broadcast_to(rstd, (CH, 128))
                v[layer, cd, :] = (xh * n2g[layer : layer + 1, :] + n2b[layer : layer + 1, :]).astype(BF)
                hu[cd, :] = mid
            pre = nn(v[layer, dst, :], fc1[layer]) + fb1[layer : layer + 1, :]
            ac, dpre = gelu_pair(pre)
            act[layer, dst, :] = ac.astype(BF)
            dp[layer, dst, :] = dpre.astype(BF)
            br = nn(ac.astype(BF), fc2[layer])
            for j in range(RT // CH):
                cd = chunk(i, j)
                h = hu[cd, :] + (br[j * CH : (j + 1) * CH] + fb2[layer : layer + 1, :])
                if layer == LAYERS - 1:
                    out_ref[cd, :] = h.astype(BF)
                else:
                    norm1(layer + 1, cd, h)
            return carry

        lax.fori_loop(0, tiles, body, 0)

    for layer in range(LAYERS):
        mix_forward(layer)
        ff_forward(layer)

    def norm_back(gv, xh, rstd, gain):
        t = gv * gain
        mt = jnp.mean(t, -1, keepdims=True)
        mx = jnp.mean(t * xh, -1, keepdims=True)
        return rstd * (t - mt - xh * mx)

    def ff_backward(layer):
        def body(i, carry):
            dst = tile(i)
            if layer == LAYERS - 1:
                g = cot_ref[dst, :].astype(F32)
            else:
                g = g_s[dst, :]
            add_to(layer, 9, g)
            gmt = g.astype(BF)
            gm[dst, :] = gmt
            gact = nt(gmt, fc2[layer])
            gpre = gact * dp[layer, dst, :].astype(F32)
            add_to(layer, 8, gpre)
            gpt = gpre.astype(BF)
            dp[layer, dst, :] = gpt
            gv = nt(gpt, fc1[layer])
            for j in range(RT // CH):
                cd = chunk(i, j)
                gvc = gv[j * CH : (j + 1) * CH]
                xh = xh2[layer, cd, :]
                add_to(layer, 6, gvc * xh)
                add_to(layer, 7, gvc)
                rstd = jnp.concatenate([rs2[layer, cd, :]] * 4, 1)
                gmc = g[j * CH : (j + 1) * CH] + norm_back(gvc, xh, rstd, n2g[layer : layer + 1, :])
                gmid[cd, :] = gmc
                gy[cd, :] = gmc.astype(BF)
            return carry

        lax.fori_loop(0, tiles, body, 0)
        base = layer * PER
        for h in range(2):
            hs = slice(h * 256, (h + 1) * 256)
            grads_ref[base + h * 256 : base + (h + 1) * 256, :] = tn(v[layer, :, hs], dp[layer]).astype(BF)
            grads_ref[base + 512 + h * 256 : base + 512 + (h + 1) * 256, :] = tn(act[layer, :, hs], gm[...]).astype(BF)

    def mix_backward(layer):
        def body(i, carry):
            dst = tile(i)
            gsr = nn(cre[dst, :], gy[...])
            gsi = nn(cim[dst, :], gy[...])
            for g in range(4):
                sl = slice(g * 128, (g + 1) * 128)
                gl = slice(g * 256, (g + 1) * 256)
                gs = jnp.concatenate([gsr[:, sl], gsi[:, sl]], 1)
                gef = gs * ds[layer, dst, gl].astype(F32)
                fe = fold(gef)
                acc[layer, 4, :, sl] += fe[:, 0:128]
                acc[layer, 5, :, sl] += fe[:, 128:256]
                geb = gef.astype(BF)
                ds[layer, dst, gl] = geb
                gaf = nt(geb, w2g[layer, g]) * da[layer, dst, gl].astype(F32)
                fa = fold(gaf)
                acc[layer, 2, :, sl] += fa[:, 0:128]
                acc[layer, 3, :, sl] += fa[:, 128:256]
                gab = gaf.astype(BF)
                da[layer, dst, gl] = gab
                gz = nt(gab, w1g[layer, g]).astype(BF)
                gzr[dst, sl] = gz[:, 0:128]
                gzi[dst, sl] = gz[:, 128:256]
            return carry

        lax.fori_loop(0, tiles, body, 0)
        base = layer * PER + 1024
        low = lax.broadcasted_iota(jnp.int32, (64, 128), 1) < 64
        for left, right, off in ((o, ds, base + 128), (z, da, base)):
            for g in range(4):
                sl = slice(g * 128, (g + 1) * 128)
                gl = slice(g * 256, (g + 1) * 256)
                p = tn(left[layer, :, gl], right[layer, :, gl])
                re = p[0:128, 0:128] + p[128:256, 128:256]
                im = p[0:128, 128:256] - p[128:256, 0:128]
                grads_ref[off : off + 64, sl] = jnp.where(low, re[0:64], re[64:128]).astype(BF)
                grads_ref[off + 64 : off + 128, sl] = jnp.where(low, im[0:64], im[64:128]).astype(BF)

    def in_backward(layer):
        def body(i, carry):
            dst = tile(i)
            y = nn(cre[dst, :], gzr[...]) + nn(cim[dst, :], gzi[...])
            for j in range(RT // CH):
                cd = chunk(i, j)
                gmc = gmid[cd, :]
                gu = y[j * CH : (j + 1) * CH] + gmc
                xh = xh1[layer, cd, :]
                add_to(layer, 0, gu * xh)
                add_to(layer, 1, gu)
                rstd = jnp.concatenate([rs1[layer, cd, :]] * 4, 1)
                gh = gmc + norm_back(gu, xh, rstd, n1g[layer : layer + 1, :])
                if layer == 0:
                    xg_ref[cd, :] = gh.astype(BF)
                else:
                    g_s[cd, :] = gh
            return carry

        lax.fori_loop(0, tiles, body, 0)

    for layer in reversed(range(LAYERS)):
        ff_backward(layer)
        mix_backward(layer)
        in_backward(layer)

    for layer in range(LAYERS):
        t = jnp.sum(acc[layer], 1)
        t = jnp.concatenate([t, jnp.zeros((6, 512), F32)], 0)
        grads_ref[layer * PER + 1280 : layer * PER + 1296, :] = t.astype(BF)


def local_step(x_in, cotangent, block_grid, keep_modes, n1g, n1b, w1, b1, w2, b2, n2g, n2b, fc1, fb1, fc2, fb2):
    rows, d = x_in.shape
    vm = pl.BlockSpec(memory_space=pltpu.VMEM)
    sm = pl.BlockSpec(memory_space=pltpu.SMEM)
    w1r = w1.reshape(LAYERS, 2, 512, 64)
    w2r = w2.reshape(LAYERS, 2, 512, 64)
    scratch = [
        pltpu.VMEM((rows, rows), BF), pltpu.VMEM((rows, rows), BF),
        pltpu.VMEM((rows, 128), F32), pltpu.VMEM((rows, 128), F32), pltpu.VMEM((rows, 128), F32),
        pltpu.VMEM((LAYERS, 4, 256, 256), BF), pltpu.VMEM((LAYERS, 4, 256, 256), BF),
        pltpu.VMEM((LAYERS, rows, d), F32), pltpu.VMEM((LAYERS, rows, 128), F32),
        pltpu.VMEM((rows, d), F32), pltpu.VMEM((rows, d), BF),
        pltpu.VMEM((LAYERS, rows, 2 * d), BF), pltpu.VMEM((LAYERS, rows, 2 * d), BF),
        pltpu.VMEM((LAYERS, rows, 2 * d), BF), pltpu.VMEM((LAYERS, rows, 2 * d), BF),
        pltpu.VMEM((rows, d), BF), pltpu.VMEM((rows, d), BF),
        pltpu.VMEM((LAYERS, rows, d), F32), pltpu.VMEM((LAYERS, rows, 128), F32),
        pltpu.VMEM((LAYERS, rows, d), BF), pltpu.VMEM((LAYERS, rows, d), BF), pltpu.VMEM((LAYERS, rows, d), BF),
        pltpu.VMEM((rows, d), BF), pltpu.VMEM((rows, d), F32),
        pltpu.VMEM((LAYERS, 10, 8, d), F32),
    ]
    return pl.pallas_call(
        kernel,
        out_shape=(
            jax.ShapeDtypeStruct((rows, d), BF),
            jax.ShapeDtypeStruct((rows, d), BF),
            jax.ShapeDtypeStruct((LAYERS * PER, d), BF),
        ),
        in_specs=[sm, sm] + [vm] * 14,
        out_specs=(vm, vm, vm),
        scratch_shapes=scratch,
        compiler_params=pltpu.CompilerParams(vmem_limit_bytes=60 * 1024 * 1024),
        name="slab_step",
    )(block_grid, keep_modes, x_in, cotangent, n1g, n1b, w1r, b1, w2r, b2, n2g, n2b, fc1, fb1, fc2, fb2)


def unpack(flat):
    per = flat.reshape(LAYERS, PER, 512).astype(F32)
    fc1g = per[:, 0:512]
    fc2g = per[:, 512:1024]

    def mix(t):
        return t.reshape(LAYERS, 2, 64, 8, 64).transpose(0, 1, 3, 2, 4)

    vec = per[:, 1280:1296]
    return (
        vec[:, 0], vec[:, 1], mix(per[:, 1024:1152]), vec[:, 2:4], mix(per[:, 1152:1280]), vec[:, 4:6],
        vec[:, 6], vec[:, 7], fc1g, vec[:, 8], fc2g, vec[:, 9],
    )


AXES = ("dp", "modes")


def exchange(a, bit, count):
    return lax.ppermute(a, AXES, [(i, i ^ bit) for i in range(count)])


def all_sum(flat, count):
    me = lax.axis_index(AXES)
    bits = [count // 2] + [1 << k for k in range((count // 2).bit_length() - 1)]
    halves = []
    for bit in bits:
        if flat.shape[0] <= 162:
            got = exchange(flat, bit, count)
            flat = (flat.astype(F32) + got.astype(F32)).astype(BF)
            continue
        n = flat.shape[0] // 2
        high = (me & bit) != 0
        low_half, high_half = flat[:n], flat[n:]
        mine = jnp.where(high, high_half, low_half)
        got = exchange(jnp.where(high, low_half, high_half), bit, count)
        flat = (mine.astype(F32) + got.astype(F32)).astype(BF)
        halves.append((bit, high))
    for bit, high in reversed(halves):
        got = exchange(flat, bit, count)
        flat = jnp.where(high, jnp.concatenate([got, flat]), jnp.concatenate([flat, got]))
    return flat


def solution(mesh):
    count = mesh.shape["dp"] * mesh.shape["modes"]

    def on_device(*args):
        out, x_grad, flat = local_step(*args)
        return (out, x_grad) + unpack(all_sum(flat, count))

    rows = P(AXES, None)
    return jax.shard_map(
        on_device,
        mesh=mesh,
        in_specs=(rows, rows, P(AXES)) + (P(),) * 13,
        out_specs=(rows, rows) + (P(),) * 12,
        check_vma=False,
    )
```

time: 1190 us -> 154 us (0.13)
  matrix products: 691 us -> 0 us
  other arithmetic: 385 us -> 6.64 us
  Pallas kernels: 0 us -> 66.8 us
  waiting for transfers between devices: 0.02 us -> 60 us
  local copies, waits for them, and re-layouts: 51.6 us -> 7.24 us
  blocking collectives: 43.7 us -> 0 us
  between operations: 15.8 us -> 0.77 us
  starting transfers between devices: 0.04 us -> 12.4 us
    dot_general x76 -> x0, matrix products: 691 us -> none  [the longest x8 479 us: synth(): jnp.einsum('srp,srd->spd', table, x.reshape(slabs, table.shape[1], -1), p...]
    dot_general x4 -> x0, other arithmetic: 234 us -> none  [spectral(): jnp.einsum('srp,spd->srd', table, x.reshape(slabs, table.shape[2], -1), p...]
    reduce_sum x17 -> x0, other arithmetic: 132 us -> none  [the longest x2 59 us: split_sums(): jnp.sum(grad_im.astype(jnp.float32), 0)]
    pallas_call x0 -> x1, Pallas kernels: none -> 66.8 us  [local_step(): pl.pallas_call(kernel, out_shape=(jax.ShapeDtypeStruct((rows, d), BF), ja...]
    ppermute x0 -> x9, waiting for transfers between devices: none -> 60 us  [exchange(): return lax.ppermute(a, AXES, [(i, i ^ bit) for i in range(count)])]
    psum x1 -> x0, blocking collectives: 43.7 us -> none  [sum_all(): lax.psum((grads[0], grads[1], grads[2], grads[3], grads[4], grads[5], gra...]
    unnamed x244 -> x2, local copies, waits for them, and re-layouts: 42.1 us -> 1.2 us
    ppermute x0 -> x9, starting transfers between devices: none -> 12.4 us  [exchange(): return lax.ppermute(a, AXES, [(i, i ^ bit) for i in range(count)])]
  transfers between devices with their start and end apart: 1 -> 9, of which waited for: 0 -> 9; matrix products, arithmetic and copies ran while one was open for 11% -> 0% of each run, Pallas kernels for 0% -> 0%
where the time goes in v1:
time: 154 us
  Pallas kernels  66.8 us (43%)
  waiting for transfers between devices  60 us (39%)
  starting transfers between devices  12.4 us (8%)
  local copies, waits for them, and re-layouts  7.24 us (5%)
  other arithmetic  6.64 us (4%)
    pallas_call x1, Pallas kernels, local_step(): pl.pallas_call(kernel, out_shape=(jax.ShapeDtypeStruct((rows, d), BF), ja...  66.8 us
    ppermute x9, waiting for transfers between devices, exchange(): return lax.ppermute(a, AXES, [(i, i ^ bit) for i in range(count)])  60 us
    ppermute x9, starting transfers between devices, exchange(): return lax.ppermute(a, AXES, [(i, i ^ bit) for i in range(count)])  12.4 us
  transfers between devices with their start and end apart: 9, of which 9 were waited for; matrix products, arithmetic and copies ran while one was open for 0% of the time, Pallas kernels for 0%

profile of v1, /device:TPU:0, one launch (start us, length us, event | category | flops | bytes accessed | tf_op | source)
XLA Modules:
  0.0 153.9 jit_solution(3981226294797189893)
XLA Ops:
  0.7 66.8 %slab_step.1 = (bf16[1024,512]{1,0:T(8,128)(2,1)}, bf16[1024,512]{1,0:T(8,128)(2,1)}, bf16[2592,512]{1,0:T(8,128)(2,1)}) custom-call(s32[16]{0:T(128)} %grid_ref.1, s32[3]{0:T(128)} %keep_ref.1, bf16[1024,512]{1,0:T(8,128)(2,1)} %x_ref.1, bf16[1024,512]{1,0:T(8,128)(2,1)} %cot_ref.1, f32[2,512]{1,0:T(2,128)} %n1g.1, f32[2,512]{1,0:T(2,128)} %n1b.1, ...), custom_call_target="tpu_custom_call" | custom-call | tf_op jit(solution)/shard_map/slab_step/pallas_call | solution.py:391
  67.5 1.9 %broadcast_select_fusion = bf16[1296,512]{1,0:T(8,128)(2,1)S(1)} fusion(pred[]{:T(512)S(6)} %ne.12, bf16[2592,512]{1,0:T(8,128)(2,1)} %get-tuple-element.19), kind=kLoop, calls=%fused_computation.4 | loop fusion | flops 663552 | bytes 3981313 | tf_op jit(solution)/shard_map/jit(_where)/select_n | solution.py:441
  69.3 0.5 collective-permute-start
  69.8 2.7 %collective-permute-done = bf16[1296,512]{1,0:T(8,128)(2,1)S(1)} collective-permute-done((bf16[1296,512]{1,0:T(8,128)(2,1)S(1)}, bf16[1296,512]{1,0:T(8,128)(2,1)S(1)}, u32[]{:S(2)}, u32[]{:S(2)}) %collective-permute-start) | collective-permute-done | bytes 1327136 | tf_op jit(solution)/shard_map/ppermute | solution.py:425
  72.5 2.3 %add_convert_fusion = bf16[1296,512]{1,0:T(8,128)(2,1)S(1)} fusion(bf16[1296,512]{1,0:T(8,128)(2,1)S(1)} %collective-permute-done, pred[]{:T(512)S(6)} %ne.12, bf16[2592,512]{1,0:T(8,128)(2,1)} %get-tuple-element.19), kind=kLoop, calls=%fused_computation.1 | loop fusion | flops 3317760 | bytes 5308417 | tf_op jit(solution)/shard_map/convert_element_type | solution.py:442
  74.8 0.1 broadcast_select_fusion.1
  74.9 2.9 %collective-permute-start.1 = (bf16[648,512]{1,0:T(8,128)(2,1)S(1)}, bf16[648,512]{1,0:T(8,128)(2,1)S(1)}, u32[]{:S(2)}, u32[]{:S(2)}) collective-permute-start(bf16[648,512]{1,0:T(8,128)(2,1)S(1)} %broadcast_select_fusion.1), channel_id=1, source_target_pairs={{0,1},{1,0},{2,3},{3,2},{4,5},{5,4},{6,7},{7,6},{8,9},{9,8},{10,11... | collective-permute-start | bytes 1990664 | tf_op jit(solution)/shard_map/ppermute | solution.py:425
  77.8 15.2 %collective-permute-done.1 = bf16[648,512]{1,0:T(8,128)(2,1)S(1)} collective-permute-done((bf16[648,512]{1,0:T(8,128)(2,1)S(1)}, bf16[648,512]{1,0:T(8,128)(2,1)S(1)}, u32[]{:S(2)}, u32[]{:S(2)}) %collective-permute-start.1) | collective-permute-done | bytes 663584 | tf_op jit(solution)/shard_map/ppermute | solution.py:425
  93.0 0.3 add_convert_fusion.1
  93.3 0.1 broadcast_select_fusion.2
  93.4 1.8 %collective-permute-start.2 = (bf16[324,512]{1,0:T(8,128)(2,1)S(1)}, bf16[324,512]{1,0:T(8,128)(2,1)S(1)}, u32[]{:S(2)}, u32[]{:S(2)}) collective-permute-start(bf16[324,512]{1,0:T(8,128)(2,1)S(1)} %broadcast_select_fusion.2), channel_id=1, source_target_pairs={{0,2},{1,3},{2,0},{3,1},{4,6},{5,7},{6,4},{7,5},{8,10},{9,11},{10,... | collective-permute-start | bytes 995336 | tf_op jit(solution)/shard_map/ppermute | solution.py:425
  95.2 7.6 %collective-permute-done.2 = bf16[324,512]{1,0:T(8,128)(2,1)S(1)} collective-permute-done((bf16[324,512]{1,0:T(8,128)(2,1)S(1)}, bf16[324,512]{1,0:T(8,128)(2,1)S(1)}, u32[]{:S(2)}, u32[]{:S(2)}) %collective-permute-start.2) | collective-permute-done | bytes 331808 | tf_op jit(solution)/shard_map/ppermute | solution.py:425
  102.8 0.2 add_convert_fusion.2
  103.1 1.6 %collective-permute-start.3 = (bf16[162,512]{1,0:T(8,128)(2,1)S(1)}, bf16[162,512]{1,0:T(8,128)(2,1)S(1)}, u32[]{:S(2)}, u32[]{:S(2)}) collective-permute-start(bf16[162,512]{1,0:T(8,128)(2,1)S(1)} %broadcast_select_fusion.3), channel_id=1, source_target_pairs={{0,4},{1,5},{2,6},{3,7},{4,0},{5,1},{6,2},{7,3},{8,12},{9,13},{10,... | collective-permute-start | bytes 497672 | tf_op jit(solution)/shard_map/ppermute | solution.py:425
  104.7 3.9 %collective-permute-done.3 = bf16[162,512]{1,0:T(8,128)(2,1)S(1)} collective-permute-done((bf16[162,512]{1,0:T(8,128)(2,1)S(1)}, bf16[162,512]{1,0:T(8,128)(2,1)S(1)}, u32[]{:S(2)}, u32[]{:S(2)}) %collective-permute-start.3) | collective-permute-done | bytes 165920 | tf_op jit(solution)/shard_map/ppermute | solution.py:425
  108.5 0.1 add_convert_fusion.4
  108.6 2.6 %collective-permute-start.4 = (bf16[162,512]{1,0:T(8,128)(2,1)S(1)}, bf16[162,512]{1,0:T(8,128)(2,1)S(1)}, u32[]{:S(2)}, u32[]{:S(2)}) collective-permute-start(bf16[162,512]{1,0:T(8,128)(2,1)S(1)} %add_convert_fusion.4), channel_id=1, source_target_pairs={{0,8},{1,9},{2,10},{3,11},{4,12},{5,13},{6,14},{7,15},{8,0},{9,1},... | collective-permute-start | bytes 497672 | tf_op jit(solution)/shard_map/ppermute | solution.py:425
  111.3 5.9 %collective-permute-done.4 = bf16[162,512]{1,0:T(8,128)(2,1)S(1)} collective-permute-done((bf16[162,512]{1,0:T(8,128)(2,1)S(1)}, bf16[162,512]{1,0:T(8,128)(2,1)S(1)}, u32[]{:S(2)}, u32[]{:S(2)}) %collective-permute-start.4) | collective-permute-done | bytes 165920 | tf_op jit(solution)/shard_map/ppermute | solution.py:425
  117.2 0.1 add_convert_fusion.3
  117.3 0.4 collective-permute-start.5
  117.6 5.1 %collective-permute-done.5 = bf16[162,512]{1,0:T(8,128)(2,1)S(1)} collective-permute-done((bf16[162,512]{1,0:T(8,128)(2,1)S(1)}, bf16[162,512]{1,0:T(8,128)(2,1)S(1)}, u32[]{:S(2)}, u32[]{:S(2)}) %collective-permute-start.5) | collective-permute-done | bytes 165920 | tf_op jit(solution)/shard_map/ppermute | solution.py:425
  122.7 0.1 maximum_select_fusion.3
  122.9 1.3 collective-permute-start.6
  124.1 6.0 %collective-permute-done.6 = bf16[324,512]{1,0:T(8,128)(2,1)S(1)} collective-permute-done((bf16[324,512]{1,0:T(8,128)(2,1)S(1)}, bf16[324,512]{1,0:T(8,128)(2,1)S(1)}, u32[]{:S(2)}, u32[]{:S(2)}) %collective-permute-start.6) | collective-permute-done | bytes 331808 | tf_op jit(solution)/shard_map/ppermute | solution.py:425
  130.1 0.3 maximum_select_fusion.2
  130.3 1.2 collective-permute-start.7
  131.6 10.6 %collective-permute-done.7 = bf16[648,512]{1,0:T(8,128)(2,1)S(1)} collective-permute-done((bf16[648,512]{1,0:T(8,128)(2,1)S(1)}, bf16[648,512]{1,0:T(8,128)(2,1)S(1)}, u32[]{:S(2)}, u32[]{:S(2)}) %collective-permute-start.7) | collective-permute-done | bytes 663584 | tf_op jit(solution)/shard_map/ppermute | solution.py:425
  142.1 0.5 maximum_select_fusion.1
  142.7 0.1 collective-permute-start.8
  142.8 3.0 %collective-permute-done.8 = bf16[1296,512]{1,0:T(8,128)(2,1)S(1)} collective-permute-done((bf16[1296,512]{1,0:T(8,128)(2,1)S(1)}, bf16[1296,512]{1,0:T(8,128)(2,1)S(1)}, u32[]{:S(2)}, u32[]{:S(2)}) %collective-permute-start.8) | collective-permute-done | bytes 1327136 | tf_op jit(solution)/shard_map/ppermute | solution.py:425
  145.8 0.8 maximum_select_fusion
  146.6 0.6 fusion.2
  147.3 0.1 fusion.3
  147.4 2.6 %fusion.1 = (f32[2,512,512]{2,1,0:T(8,128)}, f32[2,512,512]{2,1,0:T(8,128)}) fusion(bf16[2,1296,512]{2,1,0:T(8,128)(2,1)S(1)} %bitcast.23), kind=kLoop, calls=%fused_computation.22 | loop fusion | bytes 8388608 | tf_op jit(solution)/shard_map/slice | solution.py:409
  150.0 0.2 reshape.50
  150.2 0.2 reshape.49
  150.4 0.6 copy_bitcast_fusion.2
  151.0 0.6 copy_bitcast_fusion.4
  151.6 0.6 copy_bitcast_fusion.6
  152.2 1.7 %copy_bitcast_fusion = (f32[2,2,8,64,64]{4,3,2,1,0:T(8,128)}, f32[2,2,8,64,64]{4,3,2,1,0:T(8,128)}) fusion(f32[2,2,64,8,64]{4,3,2,1,0:T(8,128)S(1)} %reshape.50, f32[2,2,64,8,64]{4,3,2,1,0:T(8,128)S(1)} %reshape.49), kind=kLoop, calls=%fused_computation.5 | loop fusion | bytes 2097152 | tf_op jit(solution)/shard_map/transpose | solution.py:412
  (2 shorter events, 0.1 us)
Async XLA Ops:
  69.3 3.2 %collective-permute-start = (bf16[1296,512]{1,0:T(8,128)(2,1)S(1)}, bf16[1296,512]{1,0:T(8,128)(2,1)S(1)}, u32[]{:S(2)}, u32[]{:S(2)}) collective-permute-start(bf16[1296,512]{1,0:T(8,128)(2,1)S(1)} %broadcast_select_fusion), channel_id=1, source_target_pairs={{0,16},{1,17},{2,18},{3,19},{4,20},{5,21},{6,22},{7,23},{8,24},{9,... | collective-permute-start | bytes 3981320 | tf_op jit(solution)/shard_map/ppermute | solution.py:425
  74.9 18.1 %collective-permute-start.1 = (bf16[648,512]{1,0:T(8,128)(2,1)S(1)}, bf16[648,512]{1,0:T(8,128)(2,1)S(1)}, u32[]{:S(2)}, u32[]{:S(2)}) collective-permute-start(bf16[648,512]{1,0:T(8,128)(2,1)S(1)} %broadcast_select_fusion.1), channel_id=1, source_target_pairs={{0,1},{1,0},{2,3},{3,2},{4,5},{5,4},{6,7},{7,6},{8,9},{9,8},{10,11... | collective-permute-start | bytes 1990664 | tf_op jit(solution)/shard_map/ppermute | solution.py:425
  93.4 9.5 %collective-permute-start.2 = (bf16[324,512]{1,0:T(8,128)(2,1)S(1)}, bf16[324,512]{1,0:T(8,128)(2,1)S(1)}, u32[]{:S(2)}, u32[]{:S(2)}) collective-permute-start(bf16[324,512]{1,0:T(8,128)(2,1)S(1)} %broadcast_select_fusion.2), channel_id=1, source_target_pairs={{0,2},{1,3},{2,0},{3,1},{4,6},{5,7},{6,4},{7,5},{8,10},{9,11},{10,... | collective-permute-start | bytes 995336 | tf_op jit(solution)/shard_map/ppermute | solution.py:425
  103.1 5.5 %collective-permute-start.3 = (bf16[162,512]{1,0:T(8,128)(2,1)S(1)}, bf16[162,512]{1,0:T(8,128)(2,1)S(1)}, u32[]{:S(2)}, u32[]{:S(2)}) collective-permute-start(bf16[162,512]{1,0:T(8,128)(2,1)S(1)} %broadcast_select_fusion.3), channel_id=1, source_target_pairs={{0,4},{1,5},{2,6},{3,7},{4,0},{5,1},{6,2},{7,3},{8,12},{9,13},{10,... | collective-permute-start | bytes 497672 | tf_op jit(solution)/shard_map/ppermute | solution.py:425
  108.6 8.6 %collective-permute-start.4 = (bf16[162,512]{1,0:T(8,128)(2,1)S(1)}, bf16[162,512]{1,0:T(8,128)(2,1)S(1)}, u32[]{:S(2)}, u32[]{:S(2)}) collective-permute-start(bf16[162,512]{1,0:T(8,128)(2,1)S(1)} %add_convert_fusion.4), channel_id=1, source_target_pairs={{0,8},{1,9},{2,10},{3,11},{4,12},{5,13},{6,14},{7,15},{8,0},{9,1},... | collective-permute-start | bytes 497672 | tf_op jit(solution)/shard_map/ppermute | solution.py:425
  117.3 5.5 %collective-permute-start.5 = (bf16[162,512]{1,0:T(8,128)(2,1)S(1)}, bf16[162,512]{1,0:T(8,128)(2,1)S(1)}, u32[]{:S(2)}, u32[]{:S(2)}) collective-permute-start(bf16[162,512]{1,0:T(8,128)(2,1)S(1)} %add_convert_fusion.3), channel_id=1, source_target_pairs={{0,4},{1,5},{2,6},{3,7},{4,0},{5,1},{6,2},{7,3},{8,12},{9,13},{10,... | collective-permute-start | bytes 497672 | tf_op jit(solution)/shard_map/ppermute | solution.py:425
  122.9 7.2 %collective-permute-start.6 = (bf16[324,512]{1,0:T(8,128)(2,1)S(1)}, bf16[324,512]{1,0:T(8,128)(2,1)S(1)}, u32[]{:S(2)}, u32[]{:S(2)}) collective-permute-start(bf16[324,512]{1,0:T(8,128)(2,1)S(1)} %maximum_select_fusion.3), channel_id=1, source_target_pairs={{0,2},{1,3},{2,0},{3,1},{4,6},{5,7},{6,4},{7,5},{8,10},{9,11},{10,... | collective-permute-start | bytes 995336 | tf_op jit(solution)/shard_map/ppermute | solution.py:425
  130.3 11.8 %collective-permute-start.7 = (bf16[648,512]{1,0:T(8,128)(2,1)S(1)}, bf16[648,512]{1,0:T(8,128)(2,1)S(1)}, u32[]{:S(2)}, u32[]{:S(2)}) collective-permute-start(bf16[648,512]{1,0:T(8,128)(2,1)S(1)} %maximum_select_fusion.2), channel_id=1, source_target_pairs={{0,1},{1,0},{2,3},{3,2},{4,5},{5,4},{6,7},{7,6},{8,9},{9,8},{10,11... | collective-permute-start | bytes 1990664 | tf_op jit(solution)/shard_map/ppermute | solution.py:425
  142.7 3.1 %collective-permute-start.8 = (bf16[1296,512]{1,0:T(8,128)(2,1)S(1)}, bf16[1296,512]{1,0:T(8,128)(2,1)S(1)}, u32[]{:S(2)}, u32[]{:S(2)}) collective-permute-start(bf16[1296,512]{1,0:T(8,128)(2,1)S(1)} %maximum_select_fusion.1), channel_id=1, source_target_pairs={{0,16},{1,17},{2,18},{3,19},{4,20},{5,21},{6,22},{7,23},{8,24},{9,... | collective-permute-start | bytes 3981320 | tf_op jit(solution)/shard_map/ppermute | solution.py:425
